TPU v7x, 128 devices: a whole 4x4x4 slice. The times are simulated.
128 devices in a mesh: dp: 8 (over x, core), seq: 16 (over z, y).
Axes of the slice: x: 4, y: 4, z: 4, core: 2. Of those that a mesh axis runs over, the one named last changes fastest.
Arguments:
- trunk: bfloat16 [8, 4096, 1536], P('dp', 'seq'), may hold values from -34 to 34
- skip: bfloat16 [8, 8192, 1536], P('dp', 'seq'), may hold values from -6 to 6
- valid_bins: int32 [8], P('dp'), may hold values from 2048 to 4096, as said below
- query_weight: bfloat16 [1536, 256], replicated
- key_weight: bfloat16 [1536, 256], replicated
- value_weight: bfloat16 [1536, 768], replicated, may hold values from -0.15625 to 0.15625
- out_weight: bfloat16 [768, 1536], replicated, may hold values from -0.21875 to 0.21875
- depth_weight: float32 [3, 1536], replicated, may hold values from -3 to 3
- point_weight: bfloat16 [1536, 1536], replicated, may hold values from -0.15625 to 0.15625
- cotangent: bfloat16 [8, 8192, 1536], P('dp', 'seq'), may hold values from -6 to 6
Outputs:
- grad_pointwise: bfloat16 [1536, 1536], replicated
- grad_depthwise: float32 [3, 1536], replicated
- grad_skip: bfloat16 [8, 8192, 1536], P('dp', 'seq')
Inputs may be any that keep to these rules, and one draw needn't show every extreme that they name: Bins at or past a window's valid_bins are padding; in every draw some window is whole.
All inputs are finite; a program needn't handle non-finite values.
Results may differ from a plain program's by a relative error of at most 0.017.
Values may be sent and summed in bfloat16 or wider, within the bound.
No kernel may reach another device: no remote copies, remote signals or barrier semaphores. Data moves between devices by JAX's collectives and lax.ppermute only.
A program may use at most 128 MiB of HBM per device.

v0:
```python
from functools import partial
import math
import jax
import jax.numpy as jnp
from jax import lax
from jax.sharding import PartitionSpec as P

H = 4
DH = 64
DV = 192


def padded_2(cells, sides, width):
    for axis, dim in sides:
        count = lax.axis_size(axis)
        ends = count - 1
        head = lax.slice_in_dim(cells, 0, width, axis=dim)
        tail = lax.slice_in_dim(cells, cells.shape[dim] - width, cells.shape[dim], axis=dim)
        cells = jnp.concatenate(
            [
                lax.ppermute(tail, axis, [(i, (i + 1) % count) for i in range(ends)]),
                cells,
                lax.ppermute(head, axis, [((i + 1) % count, i) for i in range(ends)]),
            ],
            axis=dim,
        )
    return cells


def local(
    trunk,
    skip,
    valid_bins,
    query_weight,
    key_weight,
    value_weight,
    out_weight,
    depth_weight,
    point_weight,
    cotangent,
):
    tokens = trunk[0]
    row_count = tokens.shape[0]
    score_scale = 1.0 / math.sqrt(DH)
    queries = (
        jnp.dot(tokens, query_weight, preferred_element_type=jnp.float32)
        .astype(jnp.bfloat16)
        .reshape(row_count, H, DH)
    )
    keys = jnp.dot(tokens, key_weight, preferred_element_type=jnp.float32).astype(jnp.bfloat16)
    values = jnp.dot(tokens, value_weight, preferred_element_type=jnp.float32).astype(jnp.bfloat16)
    limit = valid_bins[0]
    running_max = jnp.full((H, row_count), -1e30, jnp.float32)
    weighted = jnp.zeros((row_count, H, DV), jnp.float32)
    key_piece = lax.all_gather(keys, "seq", axis=0, tiled=True)
    value_piece = lax.all_gather(values, "seq", axis=0, tiled=True)
    width = key_piece.shape[0]
    key_heads = key_piece.reshape(width, H, DH)
    value_heads = value_piece.reshape(width, H, DV)
    scores = (
        jnp.einsum("qhd,khd->hqk", queries, key_heads, preferred_element_type=jnp.float32)
        * score_scale
    )
    places = jnp.arange(width, dtype=jnp.int32)
    scores = jnp.where(places[None, None, :] < limit, scores, -1e30)
    fresh_max = jnp.maximum(running_max, jnp.max(scores, axis=2))
    shrink = jnp.exp(running_max - fresh_max)
    weights_raw = jnp.exp(scores - fresh_max[:, :, None])
    running_total = jnp.sum(weights_raw, axis=2)
    update = jnp.einsum(
        "hqk,khd->qhd",
        weights_raw.astype(jnp.bfloat16),
        value_heads,
        preferred_element_type=jnp.float32,
    )
    weighted = weighted * shrink.T[:, :, None] + update
    running_max, running_total, weighted = (fresh_max, running_total, weighted)
    mixed = (weighted / running_total.T[:, :, None]).reshape(row_count, H * DV)
    attended = (mixed * lax.rsqrt(jnp.mean(mixed * mixed, axis=1, keepdims=True) + 1e-05)).astype(
        jnp.bfloat16
    )
    hidden = (
        tokens.astype(jnp.float32)
        + jnp.dot(attended, out_weight, preferred_element_type=jnp.float32)
    ).astype(jnp.bfloat16)
    upsampled = (
        jnp.repeat(hidden, 2, axis=0).astype(jnp.float32) + skip[0].astype(jnp.float32)
    ).astype(jnp.bfloat16)
    padded = padded_2(upsampled, (("seq", 0),), 1)
    pre_act = (
        depth_weight[0] * padded[:-2]
        + depth_weight[1] * padded[1:-1]
        + depth_weight[2] * padded[2:]
    )
    act_value, pullback = jax.vjp(partial(jax.nn.gelu, approximate=True), pre_act)
    activated = act_value.astype(jnp.bfloat16)
    upstream = cotangent[0]
    grad_act = lax.dot_general(
        upstream, point_weight, (((1,), (1,)), ((), ())), preferred_element_type=jnp.float32
    )
    grad_pre = pullback(grad_act)[0].astype(jnp.bfloat16)
    fine_rows = grad_pre.shape[0]
    grad_wide = grad_pre.astype(jnp.float32)
    depth_term = jnp.stack(
        [
            jnp.sum(padded[offset : offset + fine_rows].astype(jnp.float32) * grad_wide, axis=0)
            for offset in range(3)
        ]
    )
    grad_padded = padded_2(grad_pre, (("seq", 0),), 1)
    grad_skip = (
        depth_weight[0] * grad_padded[2:]
        + depth_weight[1] * grad_padded[1:-1]
        + depth_weight[2] * grad_padded[:-2]
    ).astype(jnp.bfloat16)
    norm_scale = 1.0 / math.sqrt(lax.axis_size("dp") * lax.axis_size("seq") * fine_rows)
    point_term = lax.dot_general(
        activated, upstream, (((0,), (0,)), ((), ())), preferred_element_type=jnp.float32
    )
    point_total, depth_total = lax.psum((point_term, depth_term), ("dp", "seq"))
    grad_pointwise = (point_total * norm_scale).astype(jnp.bfloat16)
    return (grad_pointwise, depth_total * norm_scale, grad_skip[None])


def solution(mesh):
    return jax.shard_map(
        local,
        mesh=mesh,
        in_specs=(
            P("dp", "seq", None),
            P("dp", "seq", None),
            P("dp"),
            P(),
            P(),
            P(),
            P(),
            P(),
            P(),
            P("dp", "seq", None),
        ),
        out_specs=(P(), P(), P("dp", "seq", None)),
        check_vma=False,
    )
```

profile of v0, /device:TPU:1, one launch (start us, length us, event | category | flops | bytes accessed | tf_op | source)
XLA Modules:
  0.0 349.5 jit_solution(12524377417579679030)
XLA Ops:
  7.2 2.6 convolution_convert_fusion.1
  9.9 3.4 convolution_convert_fusion
  14.1 1.6 convolution_convert_fusion.2
  15.7 42.6 %all-gather.3.cloned.1.call-done = bf16[4096,256]{1,0:T(8,128)(2,1)} async-done(((bf16[256,256]{1,0:T(8,128)(2,1)}), bf16[4096,256]{1,0:T(8,128)(2,1)}) %all-gather.3.cloned.1.call-update) | async-done | bytes 2097168 | tf_op jit(solution)/shard_map/all_gather | solution.py:55
  58.2 4.1 %copy.15 = bf16[4096,256]{0,1:T(8,128)(2,1)} copy(bf16[4096,256]{1,0:T(8,128)(2,1)} %all-gather.3.cloned.1.call-done) | data formatting | bytes 4194304 | tf_op jit(solution)/shard_map/all_gather | solution.py:55
  62.3 4.1 %fusion = (f32[4,256]{1,0:T(4,128)S(1)}, f32[4,256,4096]{2,1,0:T(8,128)S(1)}) fusion(pred[4096]{0:T(1024)(128)(4,1)S(1)} %iota_compare_fusion, bf16[256,4,64]{0,2,1:T(8,128)(2,1)S(1)} %bitcast.49, bf16[4096,4,64]{0,2,1:T(8,128)(2,1)} %bitcast.47), kind=kOutput, calls=%fused_computation.2 | convolution fusion | flops 549452800 | bytes 19013632 | tf_op jit(solution)/shard_map/qhd,khd->hqk/dot_general | solution.py:61
  66.4 5.9 %copy-done.2 = f32[4,256,4096]{2,1,0:T(8,128)} copy-done((f32[4,256,4096]{2,1,0:T(8,128)}, f32[4,256,4096]{2,1,0:T(8,128)S(1)}, u32[]{:S(2)}) %copy-start.2) | copy-done | bytes 16777240
  72.4 4.0 %fusion.1 = f32[4,256]{1,0:T(4,128)S(1)} fusion(f32[4,256,4096]{2,1,0:T(8,128)S(1)} %get-tuple-element.17, f32[4,256]{1,0:T(4,128)S(1)} %get-tuple-element.15, pred[4096]{0:T(1024)(128)(4,1)S(1)} %iota_compare_fusion), kind=kLoop, calls=%fused_computation.3 | loop fusion | flops 16776192 | bytes 16789504 | tf_op jit(solution)/shard_map/reduce_sum | solution.py:69
  76.4 46.3 %all-gather.5.cloned.1.call-done = bf16[4096,768]{1,0:T(8,128)(2,1)} async-done(((bf16[256,768]{1,0:T(8,128)(2,1)}), bf16[4096,768]{1,0:T(8,128)(2,1)}) %all-gather.5.cloned.1.call-update) | async-done | bytes 6291472 | tf_op jit(solution)/shard_map/all_gather | solution.py:56
  122.7 8.6 %copy.16 = bf16[4096,768]{0,1:T(8,128)(2,1)} copy(bf16[4096,768]{1,0:T(8,128)(2,1)} %all-gather.5.cloned.1.call-done) | data formatting | bytes 12582912 | tf_op jit(solution)/shard_map/all_gather | solution.py:56
  131.3 10.3 %multiply_reduce_fusion = (f32[256]{0:T(256)S(1)}, f32[256,4,192]{0,2,1:T(8,128)S(1)}) fusion(f32[256,4]{0,1:T(4,128)S(1)} %bitcast.50, bf16[4096,4,192]{0,2,1:T(8,128)(2,1)} %bitcast.48, f32[4,256,4096]{2,1,0:T(8,128)} %copy-done.2, f32[4,256]{1,0:T(4,128)S(1)} %get-tuple-element.15, pred[4096]{0:T(1024)(128)(4,1)S(1)} %iota_compare_fusion, ...), kind=kOutput, calls=%fused_computation.68 | convolution fusion | flops 1628176128 | bytes 23872512 | tf_op jit(solution)/shard_map/hqk,khd->qhd/dot_general | solution.py:70
  142.5 2.7 broadcast_in_dim.33
  145.2 5.2 %convert_element_type.79 = f32[512,1536]{1,0:T(8,128)} reshape(f32[256,2,1536]{2,1,0:T(2,128)} %broadcast_in_dim.33) | data formatting | bytes 6291456 | tf_op jit(solution)/shard_map/convert_element_type | solution.py:87
  150.5 2.9 fusion.24
  153.4 3.1 collective-permute-start
  156.6 1.5 collective-permute-start.1
  158.1 2.8 collective-permute-done.1
  160.9 6.6 %fusion.27 = f32[1536,1536]{1,0:T(8,128)} fusion(bf16[512,1536]{1,0:T(8,128)(2,1)S(1)} %fusion.24, bf16[1,1536]{1,0:T(2,128)(2,1)S(1)} %collective-permute-done.1, bf16[1,1536]{1,0:T(2,128)(2,1)S(1)} %collective-permute-done, bf16[1,512,1536]{2,1,0:T(8,128)(2,1)S(1)} %copy-done.5, f32[1536]{0:T(1024)S(1)} %get-tuple-element.7, ...), kind=kOutput, calls=%fused_computation.41 | convolution fusion | flops 2434007040 | bytes 12607488 | tf_op jit(solution)/shard_map/dot_general | solution.py:117
  167.5 7.5 %fusion.17 = bf16[512,1536]{1,0:T(8,128)(2,1)S(1)} fusion(bf16[1,1536]{1,0:T(2,128)(2,1)S(1)} %collective-permute-done.1, bf16[512,1536]{1,0:T(8,128)(2,1)S(1)} %fusion.24, bf16[1,1536]{1,0:T(2,128)(2,1)S(1)} %collective-permute-done, bf16[1536,1536]{1,0:T(8,128)(2,1)} %param.18, bf16[1,512,1536]{2,1,0:T(8,128)(2,1)} %param.19, ...), kind=kOutput, calls=%fused_computation.28 | convolution fusion | flops 2442657792 | bytes 9461760 | tf_op jit(solution)/shard_map/dot_general | solution.py:98
  176.4 4.0 %collective-permute-start.3 = (bf16[1,1536]{1,0:T(2,128)(2,1)S(1)}, bf16[1,1536]{1,0:T(2,128)(2,1)S(1)}, u32[]{:S(2)}, u32[]{:S(2)}) collective-permute-start(bf16[1,1536]{1,0:T(2,128)(2,1)S(1)} %get-tuple-element.11), channel_id=1, source_target_pairs={{0,1},{1,2},{2,3},{3,4},{4,5},{5,6},{6,7},{7,8},{8,9},{9,10},{10,1... | collective-permute-start | bytes 9224 | tf_op jit(solution)/shard_map/ppermute | solution.py:21
  181.1 3.5 %fusion.18 = (f32[1536]{0:T(1024)S(1)}, f32[1536]{0:T(1024)S(1)}, f32[1536]{0:T(1024)S(1)}, bf16[1,512,1536]{2,1,0:T(8,128)(2,1)}) fusion(bf16[512,1536]{1,0:T(8,128)(2,1)S(1)} %fusion.17, bf16[512,1536]{1,0:T(8,128)(2,1)S(1)} %fusion.24, bf16[1,1536]{1,0:T(2,128)(2,1)S(1)} %collective-permute-done, bf16[1,1536]{1,0:T(2,128)(2,1)S(1)} %collective-permute-done.1, ...), kind=kLoop, calls=%fused_computation.29 | loop fusion | flops 23588352 | bytes 4767744 | tf_op jit(solution)/shard_map/reduce_sum | solution.py:106
  184.7 74.9 %psum.15 = f32[3,1536]{1,0:T(4,128)S(1)} all-reduce(f32[3,1536]{1,0:T(4,128)S(1)} %pad_maximum_fusion.5), channel_id=1, replica_groups=mesh['dp'=8,'seq'=16] {'dp','seq'}, use_global_device_ids=true, to_apply=%region_7.8 | all-reduce | flops 4608 | bytes 36864 | tf_op jit(solution)/shard_map/psum | solution.py:120
  260.2 75.5 %all-reduce.2.cloned.1.call-done = f32[1536,1536]{1,0:T(8,128)} async-done(((f32[1536,1536]{1,0:T(8,128)}), f32[1536,1536]{1,0:T(8,128)}) %all-reduce.2.cloned.1.call-update) | async-done | bytes 9437200 | tf_op jit(solution)/shard_map/psum | solution.py:120
  335.7 7.2 %multiply_convert_fusion = bf16[1536,1536]{1,0:T(8,128)(2,1)} fusion(f32[1536,1536]{1,0:T(8,128)} %all-reduce.2.cloned.1.call-done), kind=kLoop, calls=%fused_computation.5 | loop fusion | flops 4718592 | bytes 14155776 | tf_op jit(solution)/shard_map/convert_element_type | solution.py:121
  (34 shorter events, 3.9 us)
Async XLA Ops:
  7.2 134.5 %copy-start = (bf16[768,1536]{1,0:T(8,128)(2,1)S(1)}, bf16[768,1536]{1,0:T(8,128)(2,1)}, u32[]{:S(2)}) copy-start(bf16[768,1536]{1,0:T(8,128)(2,1)} %param.16) | copy-start | bytes 7077892
  7.2 6.9 %copy-start.3 = (bf16[1,256,1536]{2,1,0:T(8,128)(2,1)S(1)}, bf16[1,256,1536]{2,1,0:T(8,128)(2,1)}, u32[]{:S(2)}) copy-start(bf16[1,256,1536]{2,1,0:T(8,128)(2,1)} %param.10) | copy-start | bytes 2359300
  7.2 51.0 %all-gather.3.cloned.1.call-start = ((), (), s32[]{:S(2)}) async-start(), calls=%async_computation | async-start | bytes 2228224 | tf_op jit(solution)/shard_map/all_gather | solution.py:55
  9.8 112.8 %all-gather.5.cloned.1.call-start = ((), (), s32[]{:S(2)}) async-start(), calls=%async_computation.1 | async-start | bytes 6684672 | tf_op jit(solution)/shard_map/all_gather | solution.py:56
  13.4 322.4 %all-reduce.2.cloned.1.call-start = ((), (), s32[]{:S(2)}) async-start(), calls=%async_computation.2 | async-start | bytes 18874368 | tf_op jit(solution)/shard_map/psum | solution.py:120
  66.4 6.0 %copy-start.2 = (f32[4,256,4096]{2,1,0:T(8,128)}, f32[4,256,4096]{2,1,0:T(8,128)S(1)}, u32[]{:S(2)}) copy-start(f32[4,256,4096]{2,1,0:T(8,128)S(1)} %get-tuple-element.17) | copy-start | bytes 50331652
  150.5 7.6 %copy-start.4 = (f32[3,1536]{1,0:T(4,128)S(1)}, f32[3,1536]{1,0:T(4,128)}, u32[]{:S(2)}) copy-start(f32[3,1536]{1,0:T(4,128)} %param.17) | copy-start | bytes 55300
  150.5 10.4 %copy-start.5 = (bf16[1,512,1536]{2,1,0:T(8,128)(2,1)S(1)}, bf16[1,512,1536]{2,1,0:T(8,128)(2,1)}, u32[]{:S(2)}) copy-start(bf16[1,512,1536]{2,1,0:T(8,128)(2,1)} %param.19) | copy-start | bytes 4718596
  153.4 4.7 %collective-permute-start = (bf16[1,1536]{1,0:T(2,128)(2,1)S(1)}, bf16[1,1536]{1,0:T(2,128)(2,1)S(1)}, u32[]{:S(2)}, u32[]{:S(2)}) collective-permute-start(bf16[1,1536]{1,0:T(2,128)(2,1)S(1)} %get-tuple-element.12), channel_id=1, source_target_pairs={{0,1},{1,2},{2,3},{3,4},{4,5},{5,6},{6,7},{7,8},{8,9},{9,10},{10,1... | collective-permute-start | bytes 9224 | tf_op jit(solution)/shard_map/ppermute | solution.py:21
  156.6 4.4 %collective-permute-start.1 = (bf16[1,1536]{1,0:T(2,128)(2,1)S(1)}, bf16[1,1536]{1,0:T(2,128)(2,1)S(1)}, u32[]{:S(2)}, u32[]{:S(2)}) collective-permute-start(bf16[1,1536]{1,0:T(2,128)(2,1)S(1)} %get-tuple-element.13), channel_id=1, source_target_pairs={{1,0},{2,1},{3,2},{4,3},{5,4},{6,5},{7,6},{8,7},{9,8},{10,9},{11,1... | collective-permute-start | bytes 9224 | tf_op jit(solution)/shard_map/ppermute | solution.py:23
  175.1 5.3 %collective-permute-start.2 = (bf16[1,1536]{1,0:T(2,128)(2,1)S(1)}, bf16[1,1536]{1,0:T(2,128)(2,1)S(1)}, u32[]{:S(2)}, u32[]{:S(2)}) collective-permute-start(bf16[1,1536]{1,0:T(2,128)(2,1)S(1)} %get-tuple-element.10), channel_id=1, source_target_pairs={{1,0},{2,1},{3,2},{4,3},{5,4},{6,5},{7,6},{8,7},{9,8},{10,9},{11,1... | collective-permute-start | bytes 9224 | tf_op jit(solution)/shard_map/ppermute | solution.py:23
  176.4 4.8 %collective-permute-start.3 = (bf16[1,1536]{1,0:T(2,128)(2,1)S(1)}, bf16[1,1536]{1,0:T(2,128)(2,1)S(1)}, u32[]{:S(2)}, u32[]{:S(2)}) collective-permute-start(bf16[1,1536]{1,0:T(2,128)(2,1)S(1)} %get-tuple-element.11), channel_id=1, source_target_pairs={{0,1},{1,2},{2,3},{3,4},{4,5},{5,6},{6,7},{7,8},{8,9},{9,10},{10,1... | collective-permute-start | bytes 9224 | tf_op jit(solution)/shard_map/ppermute | solution.py:21
  335.7 7.2 %copy-start.1 = (bf16[768,1536]{1,0:T(8,128)(2,1)S(1)}, bf16[768,1536]{1,0:T(8,128)(2,1)}, u32[]{:S(2)}) copy-start(bf16[768,1536]{1,0:T(8,128)(2,1)} %param.16) | copy-start | bytes 7077892
Sparse Core Ops, SparseCore 0:
  10.7 47.4 all-gather.2
  60.9 61.6 all-gather.4
  167.6 168.0 all-reduce.1
where the time goes:
time: 350 us
  waiting for transfers between devices  168 us (48%)
  blocking collectives  74.9 us (21%)
  matrix products  36.9 us (11%)
  local copies, waits for them, and re-layouts  26.7 us (8%)
  other arithmetic  18.4 us (5%)
  between operations  14.6 us (4%)
  starting transfers between devices  9.98 us (3%)
    psum x1, waiting for transfers between devices, local(): point_total, depth_total = lax.psum((point_term, depth_term), ('dp', 'seq'))  75.5 us
    psum x1, blocking collectives, local(): point_total, depth_total = lax.psum((point_term, depth_term), ('dp', 'seq'))  74.9 us
    all_gather x1, waiting for transfers between devices, local(): value_piece = lax.all_gather(values, 'seq', axis=0, tiled=True)  46.3 us
    all_gather x1, waiting for transfers between devices, local(): key_piece = lax.all_gather(keys, 'seq', axis=0, tiled=True)  42.6 us
    dot_general x1, matrix products, local(): jnp.einsum('hqk,khd->qhd', weights_raw.astype(jnp.bfloat16), value_heads,...  10.3 us
    all_gather x1, local copies, waits for them, and re-layouts, local(): value_piece = lax.all_gather(values, 'seq', axis=0, tiled=True)  8.63 us
    dot_general x1, matrix products, local(): lax.dot_general(upstream, point_weight, (((1,), (1,)), ((), ())), preferr...  7.54 us
    convert_element_type x1, other arithmetic, local(): grad_pointwise = (point_total * norm_scale).astype(jnp.bfloat16)  7.24 us
  transfers between devices with their start and end apart: 7, of which 5 were waited for; matrix products, arithmetic and copies ran while one was open for 8% of the time, Pallas kernels for 0%

commit v1 on v0

--- a/solution.py
+++ b/solution.py
@@ -53,7 +53,8 @@
     running_max = jnp.full((H, row_count), -1e30, jnp.float32)
     weighted = jnp.zeros((row_count, H, DV), jnp.float32)
     key_piece = lax.all_gather(keys, "seq", axis=0, tiled=True)
-    value_piece = lax.all_gather(values, "seq", axis=0, tiled=True)
+    stack = jnp.stack([values] * lax.axis_size("seq"))
+    value_piece = jnp.concatenate(lax.all_to_all(stack, "seq", 0, 0), axis=0)
     width = key_piece.shape[0]
     key_heads = key_piece.reshape(width, H, DH)
     value_heads = value_piece.reshape(width, H, DV)

time: 350 us -> 381 us (1.089)
  local copies, waits for them, and re-layouts: 26.7 us -> 40.8 us
  waiting for transfers between devices: 168 us -> 177 us
  starting transfers between devices: 9.98 us -> 17.3 us
    all_gather x1, waiting for transfers between devices: 42.6 us -> 97.4 us  [local(): key_piece = lax.all_gather(keys, 'seq', axis=0, tiled=True)]
    all_gather x1 -> x0, waiting for transfers between devices: 46.3 us -> none  [local(): value_piece = lax.all_gather(values, 'seq', axis=0, tiled=True)]
    another operation x0 -> x2, local copies, waits for them, and re-layouts: none -> 13.7 us  [the longest x1 10.4 us: local(): value_heads = value_piece.reshape(width, H, DV)]
    all_to_all x0 -> x1, local copies, waits for them, and re-layouts: none -> 9 us  [local(): value_piece = jnp.concatenate(lax.all_to_all(stack, 'seq', 0, 0), axis=0)]
    all_to_all x0 -> x1, starting transfers between devices: none -> 8.77 us  [local(): value_piece = jnp.concatenate(lax.all_to_all(stack, 'seq', 0, 0), axis=0)]
    all_gather x1 -> x0, local copies, waits for them, and re-layouts: 8.63 us -> none  [local(): value_piece = lax.all_gather(values, 'seq', axis=0, tiled=True)]
  transfers between devices with their start and end apart: 7 -> 7, of which waited for: 5 -> 4; matrix products, arithmetic and copies ran while one was open for 8% -> 8% of each run, Pallas kernels for 0% -> 0%
where the time goes in v1:
time: 381 us
  waiting for transfers between devices  177 us (46%)
  blocking collectives  76.3 us (20%)
  local copies, waits for them, and re-layouts  40.8 us (11%)
  matrix products  36.3 us (10%)
  other arithmetic  18.4 us (5%)
  starting transfers between devices  17.3 us (5%)
  between operations  14.9 us (4%)
    all_gather x1, waiting for transfers between devices, local(): key_piece = lax.all_gather(keys, 'seq', axis=0, tiled=True)  97.4 us
    psum x1, blocking collectives, local(): point_total, depth_total = lax.psum((point_term, depth_term), ('dp', 'seq'))  76.3 us
    psum x1, waiting for transfers between devices, local(): point_total, depth_total = lax.psum((point_term, depth_term), ('dp', 'seq'))  75.4 us
    dot_general x1, matrix products, local(): jnp.einsum('hqk,khd->qhd', weights_raw.astype(jnp.bfloat16), value_heads,...  10.5 us
    another operation x1, local copies, waits for them, and re-layouts, local(): value_heads = value_piece.reshape(width, H, DV)  10.4 us
    all_to_all x1, local copies, waits for them, and re-layouts, local(): value_piece = jnp.concatenate(lax.all_to_all(stack, 'seq', 0, 0), axis=0)  9 us
    all_to_all x1, starting transfers between devices, local(): value_piece = jnp.concatenate(lax.all_to_all(stack, 'seq', 0, 0), axis=0)  8.77 us
  transfers between devices with their start and end apart: 7, of which 4 were waited for; matrix products, arithmetic and copies ran while one was open for 8% of the time, Pallas kernels for 0%

profile of v1, /device:TPU:1, one launch (start us, length us, event | category | flops | bytes accessed | tf_op | source)
XLA Modules:
  0.0 380.6 jit_solution(8857652992178612775)
XLA Ops:
  7.2 2.5 convolution_convert_fusion.1
  9.8 2.7 convolution_convert_fusion
  12.7 3.3 stack.10
  15.9 8.8 %all-to-all-start = ((bf16[16,256,768]{1,2,0:T(8,128)(2,1)}), bf16[16,256,768]{1,2,0:T(8,128)(2,1)}, u32[]{:S(2)}, u32[]{:S(2)}) async-start(bf16[16,256,768]{1,2,0:T(8,128)(2,1)} %stack.10), calls=%async_computation | async-start | bytes 12582912 | tf_op jit(solution)/shard_map/all_to_all | solution.py:57
  27.0 97.4 %all-gather.2.cloned.1.call-done = bf16[4096,256]{1,0:T(8,128)(2,1)} async-done(((bf16[256,256]{1,0:T(8,128)(2,1)}), bf16[4096,256]{1,0:T(8,128)(2,1)}) %all-gather.2.cloned.1.call-update) | async-done | bytes 2097168 | tf_op jit(solution)/shard_map/all_gather | solution.py:55
  124.5 4.1 %copy.17 = bf16[4096,256]{0,1:T(8,128)(2,1)} copy(bf16[4096,256]{1,0:T(8,128)(2,1)} %all-gather.2.cloned.1.call-done) | data formatting | bytes 4194304 | tf_op jit(solution)/shard_map/all_gather | solution.py:55
  128.5 4.1 %fusion = (f32[4,256]{1,0:T(4,128)S(1)}, f32[4,256,4096]{2,1,0:T(8,128)S(1)}) fusion(pred[4096]{0:T(1024)(128)(4,1)S(1)} %iota_compare_fusion, bf16[256,4,64]{0,2,1:T(8,128)(2,1)S(1)} %bitcast.49, bf16[4096,4,64]{0,2,1:T(8,128)(2,1)} %bitcast.48), kind=kOutput, calls=%fused_computation.2 | convolution fusion | flops 549452800 | bytes 19013632 | tf_op jit(solution)/shard_map/qhd,khd->hqk/dot_general | solution.py:62
  132.7 5.7 %copy-done.2 = f32[4,256,4096]{2,1,0:T(8,128)} copy-done((f32[4,256,4096]{2,1,0:T(8,128)}, f32[4,256,4096]{2,1,0:T(8,128)S(1)}, u32[]{:S(2)}) %copy-start.2) | copy-done | bytes 16777240
  138.4 4.0 %fusion.1 = f32[4,256]{1,0:T(4,128)S(1)} fusion(f32[4,256,4096]{2,1,0:T(8,128)S(1)} %get-tuple-element.17, f32[4,256]{1,0:T(4,128)S(1)} %get-tuple-element.15, pred[4096]{0:T(1024)(128)(4,1)S(1)} %iota_compare_fusion), kind=kLoop, calls=%fused_computation.3 | loop fusion | flops 16776192 | bytes 16789504 | tf_op jit(solution)/shard_map/reduce_sum | solution.py:70
  142.4 9.0 %copy.19 = bf16[16,256,768]{1,0,2:T(8,128)(2,1)} copy(bf16[16,256,768]{1,2,0:T(8,128)(2,1)} %all-to-all-done) | data formatting | bytes 12582912 | tf_op jit(solution)/shard_map/all_to_all | solution.py:57
  151.4 10.4 %reshape_reshape.3 = bf16[4096,4,192]{0,2,1:T(8,128)(2,1)} reshape(bf16[16,256,768]{1,0,2:T(8,128)(2,1)} %copy.19) | data formatting | bytes 12582912 | tf_op jit(solution)/shard_map/reshape;reshape | solution.py:60
  161.8 10.5 %multiply_reduce_fusion = (f32[256]{0:T(256)S(1)}, f32[256,4,192]{0,2,1:T(8,128)S(1)}) fusion(f32[256,4]{0,1:T(4,128)S(1)} %bitcast.50, bf16[4096,4,192]{0,2,1:T(8,128)(2,1)} %reshape_reshape.3, f32[4,256,4096]{2,1,0:T(8,128)} %copy-done.2, f32[4,256]{1,0:T(4,128)S(1)} %get-tuple-element.15, pred[4096]{0:T(1024)(128)(4,1)S(1)} %iota_compare_fusion, ...), kind=kOutput, calls=%fused_computation.68 | convolution fusion | flops 1628176128 | bytes 23872512 | tf_op jit(solution)/shard_map/hqk,khd->qhd/dot_general | solution.py:71
  173.2 2.7 broadcast_in_dim.33
  175.9 5.2 %convert_element_type.79 = f32[512,1536]{1,0:T(8,128)} reshape(f32[256,2,1536]{2,1,0:T(2,128)} %broadcast_in_dim.33) | data formatting | bytes 6291456 | tf_op jit(solution)/shard_map/convert_element_type | solution.py:88
  181.2 2.9 fusion.24
  184.1 1.9 collective-permute-start
  187.4 3.0 collective-permute-done.1
  190.4 6.6 %fusion.27 = f32[1536,1536]{1,0:T(8,128)} fusion(bf16[512,1536]{1,0:T(8,128)(2,1)S(1)} %fusion.24, bf16[1,1536]{1,0:T(2,128)(2,1)S(1)} %collective-permute-done.1, bf16[1,1536]{1,0:T(2,128)(2,1)S(1)} %collective-permute-done, bf16[1,512,1536]{2,1,0:T(8,128)(2,1)S(1)} %copy-done.5, f32[1536]{0:T(1024)S(1)} %get-tuple-element.7, ...), kind=kOutput, calls=%fused_computation.41 | convolution fusion | flops 2434007040 | bytes 12607488 | tf_op jit(solution)/shard_map/dot_general | solution.py:118
  197.0 7.5 %fusion.17 = bf16[512,1536]{1,0:T(8,128)(2,1)S(1)} fusion(bf16[1,1536]{1,0:T(2,128)(2,1)S(1)} %collective-permute-done.1, bf16[512,1536]{1,0:T(8,128)(2,1)S(1)} %fusion.24, bf16[1,1536]{1,0:T(2,128)(2,1)S(1)} %collective-permute-done, bf16[1536,1536]{1,0:T(8,128)(2,1)} %param.18, bf16[1,512,1536]{2,1,0:T(8,128)(2,1)} %param.19, ...), kind=kOutput, calls=%fused_computation.28 | convolution fusion | flops 2442657792 | bytes 9461760 | tf_op jit(solution)/shard_map/dot_general | solution.py:99
  205.9 4.0 %collective-permute-start.3 = (bf16[1,1536]{1,0:T(2,128)(2,1)S(1)}, bf16[1,1536]{1,0:T(2,128)(2,1)S(1)}, u32[]{:S(2)}, u32[]{:S(2)}) collective-permute-start(bf16[1,1536]{1,0:T(2,128)(2,1)S(1)} %get-tuple-element.11), channel_id=1, source_target_pairs={{0,1},{1,2},{2,3},{3,4},{4,5},{5,6},{6,7},{7,8},{8,9},{9,10},{10,1... | collective-permute-start | bytes 9224 | tf_op jit(solution)/shard_map/ppermute | solution.py:21
  210.6 3.5 fusion.18
  214.2 76.3 %psum.15 = f32[3,1536]{1,0:T(4,128)S(1)} all-reduce(f32[3,1536]{1,0:T(4,128)S(1)} %pad_maximum_fusion.5), channel_id=1, replica_groups=mesh['dp'=8,'seq'=16] {'dp','seq'}, use_global_device_ids=true, to_apply=%region_7.8 | all-reduce | flops 4608 | bytes 36864 | tf_op jit(solution)/shard_map/psum | solution.py:121
  291.1 75.4 %all-reduce.2.cloned.1.call-done = f32[1536,1536]{1,0:T(8,128)} async-done(((f32[1536,1536]{1,0:T(8,128)}), f32[1536,1536]{1,0:T(8,128)}) %all-reduce.2.cloned.1.call-update) | async-done | bytes 9437200 | tf_op jit(solution)/shard_map/psum | solution.py:121
  366.5 7.2 %multiply_convert_fusion = bf16[1536,1536]{1,0:T(8,128)(2,1)} fusion(f32[1536,1536]{1,0:T(8,128)} %all-reduce.2.cloned.1.call-done), kind=kLoop, calls=%fused_computation.5 | loop fusion | flops 4718592 | bytes 14155776 | tf_op jit(solution)/shard_map/convert_element_type | solution.py:122
  (36 shorter events, 6.8 us)
Async XLA Ops:
  7.2 165.2 %copy-start = (bf16[768,1536]{1,0:T(8,128)(2,1)S(1)}, bf16[768,1536]{1,0:T(8,128)(2,1)}, u32[]{:S(2)}) copy-start(bf16[768,1536]{1,0:T(8,128)(2,1)} %param.16) | copy-start | bytes 7077892
  7.2 117.3 %all-gather.2.cloned.1.call-start = ((), (), s32[]{:S(2)}) async-start(), calls=%async_computation.1 | async-start | bytes 2228224 | tf_op jit(solution)/shard_map/all_gather | solution.py:55
  15.9 9.5 %copy-start.3 = (bf16[1,256,1536]{2,1,0:T(8,128)(2,1)S(1)}, bf16[1,256,1536]{2,1,0:T(8,128)(2,1)}, u32[]{:S(2)}) copy-start(bf16[1,256,1536]{2,1,0:T(8,128)(2,1)} %param.10) | copy-start | bytes 2359300
  15.9 126.4 %all-to-all-start = ((bf16[16,256,768]{1,2,0:T(8,128)(2,1)}), bf16[16,256,768]{1,2,0:T(8,128)(2,1)}, u32[]{:S(2)}, u32[]{:S(2)}) async-start(bf16[16,256,768]{1,2,0:T(8,128)(2,1)} %stack.10), calls=%async_computation | async-start | bytes 12582912 | tf_op jit(solution)/shard_map/all_to_all | solution.py:57
  24.7 341.8 %all-reduce.2.cloned.1.call-start = ((), (), s32[]{:S(2)}) async-start(), calls=%async_computation.2 | async-start | bytes 18874368 | tf_op jit(solution)/shard_map/psum | solution.py:121
  132.6 5.7 %copy-start.2 = (f32[4,256,4096]{2,1,0:T(8,128)}, f32[4,256,4096]{2,1,0:T(8,128)S(1)}, u32[]{:S(2)}) copy-start(f32[4,256,4096]{2,1,0:T(8,128)S(1)} %get-tuple-element.17) | copy-start | bytes 50331652
  181.2 6.2 %copy-start.4 = (f32[3,1536]{1,0:T(4,128)S(1)}, f32[3,1536]{1,0:T(4,128)}, u32[]{:S(2)}) copy-start(f32[3,1536]{1,0:T(4,128)} %param.17) | copy-start | bytes 55300
  181.2 9.3 %copy-start.5 = (bf16[1,512,1536]{2,1,0:T(8,128)(2,1)S(1)}, bf16[1,512,1536]{2,1,0:T(8,128)(2,1)}, u32[]{:S(2)}) copy-start(bf16[1,512,1536]{2,1,0:T(8,128)(2,1)} %param.19) | copy-start | bytes 4718596
  184.1 3.3 collective-permute-start
  186.1 4.4 %collective-permute-start.1 = (bf16[1,1536]{1,0:T(2,128)(2,1)S(1)}, bf16[1,1536]{1,0:T(2,128)(2,1)S(1)}, u32[]{:S(2)}, u32[]{:S(2)}) collective-permute-start(bf16[1,1536]{1,0:T(2,128)(2,1)S(1)} %get-tuple-element.13), channel_id=1, source_target_pairs={{1,0},{2,1},{3,2},{4,3},{5,4},{6,5},{7,6},{8,7},{9,8},{10,9},{11,1... | collective-permute-start | bytes 9224 | tf_op jit(solution)/shard_map/ppermute | solution.py:23
  204.6 5.3 %collective-permute-start.2 = (bf16[1,1536]{1,0:T(2,128)(2,1)S(1)}, bf16[1,1536]{1,0:T(2,128)(2,1)S(1)}, u32[]{:S(2)}, u32[]{:S(2)}) collective-permute-start(bf16[1,1536]{1,0:T(2,128)(2,1)S(1)} %get-tuple-element.10), channel_id=1, source_target_pairs={{1,0},{2,1},{3,2},{4,3},{5,4},{6,5},{7,6},{8,7},{9,8},{10,9},{11,1... | collective-permute-start | bytes 9224 | tf_op jit(solution)/shard_map/ppermute | solution.py:23
  205.9 4.8 %collective-permute-start.3 = (bf16[1,1536]{1,0:T(2,128)(2,1)S(1)}, bf16[1,1536]{1,0:T(2,128)(2,1)S(1)}, u32[]{:S(2)}, u32[]{:S(2)}) collective-permute-start(bf16[1,1536]{1,0:T(2,128)(2,1)S(1)} %get-tuple-element.11), channel_id=1, source_target_pairs={{0,1},{1,2},{2,3},{3,4},{4,5},{5,6},{6,7},{7,8},{8,9},{9,10},{10,1... | collective-permute-start | bytes 9224 | tf_op jit(solution)/shard_map/ppermute | solution.py:21
  366.5 7.2 %copy-start.1 = (bf16[768,1536]{1,0:T(8,128)(2,1)S(1)}, bf16[768,1536]{1,0:T(8,128)(2,1)}, u32[]{:S(2)}) copy-start(bf16[768,1536]{1,0:T(8,128)(2,1)} %param.16) | copy-start | bytes 7077892
Sparse Core Ops, SparseCore 0:
  10.7 113.6 all-gather.1
  197.1 169.3 all-reduce.1
